TPU v7x, 32 devices: a whole 2x2x4 slice. The times are simulated.
32 devices in a mesh: req: 4 (over y, core), blk: 8 (over z, x).
Axes of the slice: x: 2, y: 2, z: 4, core: 2. Of those that a mesh axis runs over, the one named last changes fastest.
Arguments:
- queries: bfloat16 [512, 8192], P('req', 'blk'), may hold values from -120 to 120
- suffix_key_value: bfloat16 [512, 8, 256], P('req'), may hold values from -6 to 6
- residual: bfloat16 [512, 8192], P('req', 'blk'), may hold values from -10 to 10
- gain: float32 [8192], P('blk'), may hold values from 0.1 to 1.9
- gate_up: bfloat16 [8192, 2, 14336], P('blk', None, 'req'), may hold values from -0.0625 to 0.0625
- prefix_cache_slots: bfloat16 [32, 128, 8, 256], P('req'), may hold values from -6 to 6
- prefix_page_slots: int32 [32], replicated, may hold values from 0 to 31, each once
- lengths: int32 [4, 4], replicated, may hold values from 1 to 64, 128 in all within a row
- counts: int32 [4], replicated, may hold values from 1 to 32, as said below
Outputs:
- hidden: bfloat16 [512, 14336], P('blk', 'req')
- suffix_cache: bfloat16 [512, 2048], P('req', 'blk')
Inputs may be any that keep to these rules, and one draw needn't show every extreme that they name: `prefix_page_slots`: slot s of prefix_cache_slots lies on index s // 8 of req; every slot holds exactly one page. Each group's lengths sum to 128, and each group has one request of exactly 64 tokens. `counts`: some group reads all 32 pages.
All inputs are finite; a program needn't handle non-finite values.
Results may differ from a plain program's by a relative error of at most 0.034.
Values may be sent and summed in bfloat16 or wider, within the bound.
No kernel may reach another device: no remote copies, remote signals or barrier semaphores. Data moves between devices by JAX's collectives and lax.ppermute only.
A program may use at most 256 MiB of HBM per device.

v0:
```python
import math

import jax
import jax.numpy as jnp
from jax import lax
from jax.sharding import PartitionSpec as P

D = 8192


NEGATIVE = -1e30
EPSILON = 1e-05
ROPE_BASE = 500000.0


def rope_tables(positions, half_dim):
    inverse = jnp.exp(
        -math.log(ROPE_BASE) * jnp.arange(half_dim, dtype=jnp.float32) * 2.0 / (2 * half_dim)
    )
    angles = positions.astype(jnp.float32)[:, None] * inverse[None, :]
    return (jnp.cos(angles), jnp.sin(angles))


def rotate(vectors, cosines, sines):
    half_dim = vectors.shape[-1] // 2
    lower = vectors[..., :half_dim]
    upper = vectors[..., half_dim:]
    return jnp.concatenate([lower * cosines - upper * sines, upper * cosines + lower * sines], -1)


def suffix_layout(lengths_row, page_count, group_len, page_len):
    starts = jnp.cumsum(lengths_row) - lengths_row
    tokens_at = jnp.arange(group_len, dtype=jnp.int32)
    request = jnp.sum((tokens_at[:, None] >= starts[None, :]).astype(jnp.int32), 1) - 1
    slots_req = jnp.arange(lengths_row.shape[0], dtype=jnp.int32)
    request_begin = jnp.sum(
        jnp.where(request[:, None] == slots_req[None, :], starts[None, :], 0), 1
    )
    offset = tokens_at - request_begin
    return (request, offset, page_count * page_len + offset)


def absorb(state, query, keys_in, values_in, usable, score_scale):
    weighted, running_max, weight_sum = state
    scores = (
        jnp.einsum("tqd,nd->tqn", query, keys_in, preferred_element_type=jnp.float32) * score_scale
    )
    scores = jnp.where(usable, scores, NEGATIVE)
    new_max = jnp.maximum(running_max, jnp.max(scores, -1))
    probs = jnp.where(usable, jnp.exp(scores - new_max[..., None]), 0.0)
    factor = jnp.exp(running_max - new_max)
    weight_sum = weight_sum * factor + jnp.sum(probs, -1)
    weighted = weighted * factor[..., None] + jnp.einsum(
        "tqn,nd->tqd", probs.astype(jnp.bfloat16), values_in, preferred_element_type=jnp.float32
    )
    return (weighted, new_max, weight_sum)


def absorb_pages(state, query, pages_in, page_numbers, limit, score_scale):
    n_pages, page_len, lanes = pages_in.shape
    head_dim = lanes // 2
    key_target = max(page_len, (1 << 20) // (query.shape[0] * query.shape[1]))
    per_block = math.gcd(n_pages, max(1, key_target // page_len))
    n_blocks = n_pages // per_block

    def step(index, carry):
        block = lax.dynamic_slice_in_dim(pages_in, index * per_block, per_block, 0).reshape(
            per_block * page_len, lanes
        )
        numbers = lax.dynamic_slice_in_dim(page_numbers, index * per_block, per_block, 0)
        usable = jnp.repeat(numbers, page_len)[None, None, :] < limit
        return absorb(carry, query, block[:, :head_dim], block[:, head_dim:], usable, score_scale)

    return lax.fori_loop(0, n_blocks, step, state)


def empty_state(rows_count, heads_here, head_dim):
    return (
        jnp.zeros((rows_count, heads_here, head_dim), jnp.float32),
        jnp.full((rows_count, heads_here), NEGATIVE, jnp.float32),
        jnp.zeros((rows_count, heads_here), jnp.float32),
    )


def on_device(
    queries,
    suffix_key_value,
    residual,
    gain,
    gate_up,
    prefix_cache_slots,
    prefix_page_slots,
    lengths,
    counts,
):
    blocks = lax.axis_size("blk")
    column = lax.axis_index("blk")
    group_index = lax.axis_index("req")
    group_len = queries.shape[0]
    heads_kv = suffix_key_value.shape[1]
    head_dim = suffix_key_value.shape[2] // 2
    heads_here = queries.shape[1] // head_dim
    page_len = prefix_cache_slots.shape[1]
    score_scale = 1.0 / math.sqrt(head_dim)
    kv_head = column * heads_kv // blocks
    page_count = counts[group_index]
    request, offset, positions = suffix_layout(
        lengths[group_index], page_count, group_len, page_len
    )
    cosines, sines = rope_tables(positions, head_dim // 2)
    rotated_query = rotate(
        queries.astype(jnp.float32).reshape(group_len, heads_here, head_dim),
        cosines[:, None],
        sines[:, None],
    ).astype(jnp.bfloat16)
    own_head = lax.dynamic_index_in_dim(suffix_key_value, kv_head, 1, keepdims=False)
    keys_new = rotate(own_head[:, :head_dim].astype(jnp.float32), cosines, sines).astype(
        jnp.bfloat16
    )
    values_new = own_head[:, head_dim:]
    both_new = jnp.concatenate([keys_new, values_new], 1)
    lane_width = 2 * heads_kv * head_dim // blocks
    updated_cache = lax.dynamic_slice_in_dim(
        both_new, column * lane_width % (2 * head_dim), lane_width, 1
    )
    allowed = (request[:, None] == request[None, :]) & (offset[None, :] <= offset[:, None])
    state = absorb(
        empty_state(group_len, heads_here, head_dim),
        rotated_query,
        keys_new,
        values_new,
        allowed[:, None, :],
        score_scale,
    )
    pages_total = prefix_page_slots.shape[0]
    page_ids = jnp.arange(pages_total, dtype=jnp.int32)
    own_slots = lax.dynamic_index_in_dim(prefix_cache_slots, kv_head, 2, keepdims=False)
    shard_piece = lax.all_gather(own_slots, "req", axis=0, tiled=True)
    slot_ids = jnp.arange(shard_piece.shape[0], dtype=jnp.int32)
    match = prefix_page_slots[None, :] == slot_ids[:, None]
    state = absorb_pages(
        state,
        rotated_query,
        shard_piece,
        jnp.sum(jnp.where(match, page_ids[None, :], 0), 1),
        page_count,
        score_scale,
    )
    attention_output = (state[0] / state[2][..., None]).reshape(group_len, heads_here * head_dim)
    stream = (residual.astype(jnp.float32) + attention_output).astype(jnp.bfloat16)
    stream_f32 = stream.astype(jnp.float32)
    square_sum = lax.psum(jnp.sum(stream_f32 * stream_f32, 1), "blk")
    normed = (stream_f32 * lax.rsqrt(square_sum[:, None] / D + EPSILON) * gain[None, :]).astype(
        jnp.bfloat16
    )
    gathered = lax.all_gather(normed, "req", axis=0, tiled=True)
    weights = gate_up.reshape(gate_up.shape[0], 2 * gate_up.shape[2])
    width_here = gate_up.shape[2]
    summed = lax.psum_scatter(
        jnp.dot(gathered, weights, preferred_element_type=jnp.float32).astype(jnp.bfloat16),
        "blk",
        scatter_dimension=0,
        tiled=True,
    ).astype(jnp.float32)
    hidden = (jax.nn.silu(summed[:, :width_here]) * summed[:, width_here:]).astype(jnp.bfloat16)
    return (hidden, updated_cache)


def solution(mesh):
    placed = (
        P("req", "blk"),
        P("req", None, None),
        P("req", "blk"),
        P("blk"),
        P("blk", None, "req"),
        P("req", None, None, None),
        P(),
        P(),
        P(),
    )
    return jax.shard_map(
        on_device,
        mesh=mesh,
        in_specs=placed,
        out_specs=(P("blk", "req"), P("req", "blk")),
        check_vma=False,
    )
```

profile of v0, /device:TPU:0, one launch (start us, length us, event | category | flops | bytes accessed | tf_op | source)
XLA Modules:
  0.0 251.8 jit_solution(8818321400212933685)
XLA Ops:
  7.2 0.0 copy-start
  7.2 0.0 copy-start.5
  7.2 0.0 copy-start.6
  7.2 0.0 all-gather.6.cloned.1.call-start
  7.3 3.4 %constant_dynamic-slice_fusion.2 = bf16[8,128,1,256]{3,2,1,0:T(2,128)(2,1)S(1)} fusion(bf16[8,128,8,256]{3,2,1,0:T(8,128)(2,1)} %param.16, s32[]{:T(128)S(6)} %select_n.64), kind=kLoop, calls=%fused_computation.66 | loop fusion | bytes 1048580 | tf_op jit(solution)/shard_map/jit(dynamic_index_in_dim)/dynamic_slice | solution.py:137
  10.7 0.9 copy.46
  11.6 0.0 all-gather.6.cloned.1.call-update
  11.6 0.0 all-gather.4.cloned.1.call-start
  11.7 0.1 select_reduce_fusion
  11.8 0.6 dynamic_slice.30
  12.4 0.2 reduce-window_clone.1
  12.6 0.1 constant_dynamic-slice_fusion.1
  12.7 0.2 copy.33
  12.9 0.2 copy.34
  13.1 0.2 copy.44
  13.3 0.2 copy.43
  14.2 0.1 convert_reduce_fusion
  14.3 0.1 select_reduce_fusion.1
  14.4 0.3 subtract_convert_fusion.1
  14.8 0.1 subtract_convert_fusion
  14.9 0.1 pad_maximum_fusion
  15.1 0.1 compare_and_fusion
  15.2 0.3 fusion.36
  15.5 0.1 fusion.21
  15.6 0.3 convolution_add_fusion
  15.9 21.1 %all-gather.6.cloned.1.call-done = bf16[32,128,1,256]{3,1,2,0:T(8,128)(2,1)} async-done(((bf16[8,128,1,256]{3,1,2,0:T(8,128)(2,1)}), bf16[32,128,1,256]{3,1,2,0:T(8,128)(2,1)}) %all-gather.6.cloned.1.call-update) | async-done | bytes 2097168 | tf_op jit(solution)/shard_map/all_gather | solution.py:138
  37.1 23.8 %while.17 = (s32[]{:T(128)}, f32[128,8,128]{2,0,1:T(8,128)S(1)}, f32[128,8]{0,1:T(8,128)S(1)}, f32[128,8]{0,1:T(8,128)S(1)}, s32[32]{0:T(128)S(1)}, /*index=5*/s...) while((s32[]{:T(128)}, f32[128,8,128]{2,0,1:T(8,128)S(1)}, ...), condition=%wide.region_9.10_spmd, body=%wide.region_6.9_spmd.sunk | while | flops 550766592 | bytes 15537375 | solution.py:74
  37.1 0.7 dynamic-slice_compare_fusion.2
  37.8 0.1 broadcast_bitcast_fusion.2
  37.9 1.1 constant_dynamic-slice_fusion.5
  39.0 0.7 bitcast_reduce_fusion.2
  39.7 1.4 fusion.47
  41.2 1.8 fusion.48
  43.0 0.7 dynamic-slice_compare_fusion.2
  43.8 0.1 broadcast_bitcast_fusion.2
  43.8 1.1 constant_dynamic-slice_fusion.5
  44.9 0.7 bitcast_reduce_fusion.2
  45.7 1.4 fusion.47
  47.1 1.8 fusion.48
  49.0 0.7 dynamic-slice_compare_fusion.2
  49.7 0.1 broadcast_bitcast_fusion.2
  49.8 1.1 constant_dynamic-slice_fusion.5
  50.9 0.7 bitcast_reduce_fusion.2
  51.6 1.4 fusion.47
  53.1 1.8 fusion.48
  54.9 0.7 dynamic-slice_compare_fusion.2
  55.7 0.1 broadcast_bitcast_fusion.2
  55.7 1.1 constant_dynamic-slice_fusion.5
  56.8 0.8 bitcast_reduce_fusion.2
  57.6 1.4 fusion.47
  59.0 1.8 fusion.48
  60.9 0.2 copy.40
  61.2 0.2 fusion.17
  61.3 21.4 %psum.7 = f32[128]{0:T(128)S(1)} all-reduce(f32[128]{0:T(128)S(1)} %fusion.17), channel_id=1, replica_groups=mesh['req'=4,'blk'=8] {'blk'}, use_global_device_ids=true, to_apply=%region_11.12 | all-reduce | flops 128 | bytes 1024 | tf_op jit(solution)/shard_map/psum | solution.py:152
  82.7 0.9 fusion.19
  83.6 0.0 all-gather.4.cloned.1.call-update
  83.6 0.2 reduce-scatter.2.cloned.1.call-start
  83.9 15.8 %copy.47 = bf16[128,8,2,3584]{3,1,2,0:T(8,128)(2,1)} copy(bf16[128,8,2,3584]{3,2,1,0:T(2,128)(2,1)} %bitcast.74) | data formatting | bytes 29360128
  99.7 13.2 %convolution_convert_fusion = bf16[512,7168]{1,0:T(8,128)(2,1)} fusion(bf16[512,1024]{0,1:T(8,128)(2,1)} %all-gather.4.cloned.1.call-done, bf16[1024,7168]{1,0:T(8,128)(2,1)} %bitcast.75), kind=kOutput, calls=%fused_computation.22 | convolution fusion | flops 7519862784 | bytes 23068672 | tf_op jit(solution)/shard_map/dot_general | solution.py:160
  112.9 0.0 reduce-scatter.2.cloned.1.call-update
  112.9 0.7 pad_maximum_fusion.1
  113.6 129.3 %reduce-scatter.2.cloned.1.call-done = bf16[64,7168]{1,0:T(8,128)(2,1)} async-done(((bf16[512,7168]{1,0:T(8,128)(2,1)}), bf16[64,7168]{1,0:T(8,128)(2,1)}) %reduce-scatter.2.cloned.1.call-update) | async-done | bytes 917520 | tf_op jit(solution)/shard_map/reduce_scatter | solution.py:159
  243.0 1.3 convert_element_type.56
  244.3 1.0 fusion.16
  (36 shorter events, 0.3 us)
Async XLA Ops:
  7.2 5.4 %copy-start = (bf16[128,8,256]{2,1,0:T(8,128)(2,1)S(1)}, bf16[128,8,256]{2,1,0:T(8,128)(2,1)}, u32[]{:S(2)}) copy-start(bf16[128,8,256]{2,1,0:T(8,128)(2,1)} %param.12) | copy-start | bytes 1572868
  7.2 4.5 %copy-start.5 = (s32[32]{0:T(128)S(1)}, s32[32]{0:T(128)}, u32[]{:S(2)}) copy-start(s32[32]{0:T(128)} %param.17) | copy-start | bytes 388
  7.2 4.6 %copy-start.6 = (s32[4]{0:T(128)S(1)}, s32[4]{0:T(128)}, u32[]{:S(2)}) copy-start(s32[4]{0:T(128)} %param.19) | copy-start | bytes 52
  7.2 5.2 %copy-start.4 = (s32[4,4]{1,0:T(4,128)S(1)}, s32[4,4]{1,0:T(4,128)}, u32[]{:S(2)}) copy-start(s32[4,4]{1,0:T(4,128)} %param.18) | copy-start | bytes 196
  7.2 5.5 %copy-start.1 = (bf16[128,1024]{1,0:T(8,128)(2,1)S(1)}, bf16[128,1024]{1,0:T(8,128)(2,1)}, u32[]{:S(2)}) copy-start(bf16[128,1024]{1,0:T(8,128)(2,1)} %param.13) | copy-start | bytes 786436
  7.2 5.7 %copy-start.2 = (bf16[128,1024]{1,0:T(8,128)(2,1)S(1)}, bf16[128,1024]{1,0:T(8,128)(2,1)}, u32[]{:S(2)}) copy-start(bf16[128,1024]{1,0:T(8,128)(2,1)} %param.11) | copy-start | bytes 786436
  7.2 29.8 %all-gather.6.cloned.1.call-start = ((), (), s32[]{:S(2)}) async-start(), calls=%async_computation.3 | async-start | bytes 2621440 | tf_op jit(solution)/shard_map/all_gather | solution.py:138
  11.6 88.1 %all-gather.4.cloned.1.call-start = ((), (), s32[]{:S(2)}) async-start(), calls=%async_computation.1 | async-start | bytes 1310720 | tf_op jit(solution)/shard_map/all_gather | solution.py:156
  37.1 45.6 %copy-start.3 = (f32[1024]{0:T(1024)S(1)}, f32[1024]{0:T(1024)}, u32[]{:S(2)}) copy-start(f32[1024]{0:T(1024)} %param.14) | copy-start | bytes 12292
  83.6 159.4 %reduce-scatter.2.cloned.1.call-start = ((), (), s32[]{:S(2)}) async-start(), calls=%async_computation.2 | async-start | bytes 8257536 | tf_op jit(solution)/shard_map/reduce_scatter | solution.py:159
Sparse Core Ops, SparseCore 0:
  11.7 25.3 all-gather.5
  83.7 13.1 all-gather.3
  113.0 129.9 reduce-scatter.1
where the time goes:
time: 252 us
  waiting for transfers between devices  151 us (60%)
  local copies, waits for them, and re-layouts  26.5 us (11%)
  matrix products  24.1 us (10%)
  blocking collectives  21.4 us (8%)
  between operations  14.7 us (6%)
  other arithmetic  14.2 us (6%)
    reduce_scatter x1, waiting for transfers between devices, on_device(): lax.psum_scatter(jnp.dot(gathered, weights, preferred_element_type=jnp.fl...  129 us
    psum x1, blocking collectives, on_device(): square_sum = lax.psum(jnp.sum(stream_f32 * stream_f32, 1), 'blk')  21.4 us
    all_gather x1, waiting for transfers between devices, on_device(): shard_piece = lax.all_gather(own_slots, 'req', axis=0, tiled=True)  21.1 us
    unnamed x21, local copies, waits for them, and re-layouts  17.5 us
    dot_general x1, matrix products, on_device(): jnp.dot(gathered, weights, preferred_element_type=jnp.float32)  13.2 us
    dot_general x5, matrix products, absorb(): jnp.einsum('tqn,nd->tqd', probs.astype(jnp.bfloat16), values_in, preferre...  7.63 us
    reduce_sum x5, other arithmetic, absorb(): weight_sum = weight_sum * factor + jnp.sum(probs, -1)  5.78 us
  transfers between devices with their start and end apart: 3, of which 2 were waited for; matrix products, arithmetic and copies ran while one was open for 8% of the time, Pallas kernels for 0%

commit v1 on v0

v1 whole, which is shorter than its diff:
```python
import functools
import math

import jax
import jax.numpy as jnp
from jax import lax
from jax.experimental import pallas as pl
from jax.experimental.pallas import tpu as pltpu
from jax.sharding import PartitionSpec as P

D = 8192


NEGATIVE = -1e30
EPSILON = 1e-05
ROPE_BASE = 500000.0
ROW_BLOCK = 256
CHUNKS = ((6, (0, 2, 1)), (6, (1, 0, 2)), (6, (0, 2, 1)), (4, (1, 0, 2)), (4, (0, 1, 2)), (2, (1, 0, 2)))
STEPS = ("S0", "S1", "S2", "S3", "S4", "K0", "K1", "S5", "K2", "K3", "K4", "A0", "A1", "K5", "Q0", "A2", "A3", "Q1", "A4", "A5", "Q2", "F0", "F1", "F2", "F3", "F4", "F5")


def rope_tables(positions, half_dim):
    inverse = jnp.exp(
        -math.log(ROPE_BASE) * jnp.arange(half_dim, dtype=jnp.float32) * 2.0 / (2 * half_dim)
    )
    angles = positions.astype(jnp.float32)[:, None] * inverse[None, :]
    cosines, sines = jnp.cos(angles), jnp.sin(angles)
    return (jnp.concatenate([cosines, cosines], 1), jnp.concatenate([-sines, sines], 1))


def suffix_layout(lengths_row, page_count, group_len, page_len):
    starts = jnp.cumsum(lengths_row) - lengths_row
    tokens_at = jnp.arange(group_len, dtype=jnp.int32)
    request = jnp.sum((tokens_at[:, None] >= starts[None, :]).astype(jnp.int32), 1) - 1
    slots_req = jnp.arange(lengths_row.shape[0], dtype=jnp.int32)
    request_begin = jnp.sum(
        jnp.where(request[:, None] == slots_req[None, :], starts[None, :], 0), 1
    )
    offset = tokens_at - request_begin
    return (request, offset, page_count * page_len + offset)


def dot_nt(a, b):
    return lax.dot_general(a, b, (((1,), (1,)), ((), ())), preferred_element_type=jnp.float32)


def rotate(vectors, cosines, signed_sines):
    half_dim = vectors.shape[-1] // 2
    return vectors * cosines + pltpu.roll(vectors, half_dim, 1) * signed_sines


def absorb(items, query, scale, acc, top, total):
    def scores_of(item):
        rows, keys, _, bias = item
        scores = dot_nt(query[rows, :], keys()) * scale
        return scores if bias is None else scores + bias

    scores = scores_of(items[0])
    for i, (rows, _, values, _) in enumerate(items):
        ahead = scores_of(items[i + 1]) if i + 1 < len(items) else None
        old_top = top[rows, :]
        new_top = jnp.maximum(old_top, jnp.max(scores, 1, keepdims=True))
        weights = jnp.exp2(scores - new_top[:, :1])
        factor = jnp.exp2(old_top - new_top)
        top[rows, :] = new_top
        lanes = top.shape[1]
        part = weights[:, :lanes]
        for begin in range(lanes, weights.shape[1], lanes):
            part = part + weights[:, begin : begin + lanes]
        total[rows, :] = total[rows, :] * factor + part
        acc[rows, :] = acc[rows, :] * factor + jnp.dot(
            weights.astype(jnp.bfloat16), values(), preferred_element_type=jnp.float32
        )
        scores = ahead


def absorb_pages(shards, meta, page_len, query, scale, acc, top, total):
    head_dim = query.shape[1]
    rows = query.shape[0]
    row_step = min(ROW_BLOCK, rows)
    keys_here = shards[0].shape[0]
    pages = keys_here // page_len
    count = meta[0]
    visible = [meta[1 + i] < count for i in range(len(shards) * pages)]
    every = functools.reduce(jnp.logical_and, visible)

    def items_of(shard, begin, length, bias):
        return [
            (
                pl.ds(r, row_step),
                lambda: shard[pl.ds(begin, length), :head_dim],
                lambda: shard[pl.ds(begin, length), head_dim:],
                bias,
            )
            for r in range(0, rows, row_step)
        ]

    @pl.when(every)
    def _():
        items = []
        for shard in shards:
            items += items_of(shard, 0, keys_here, None)
        absorb(items, query, scale, acc, top, total)

    per_block = min(4, pages)
    length = per_block * page_len
    lane = lax.broadcasted_iota(jnp.int32, (1, length), 1) // page_len
    for s, shard in enumerate(shards):
        for begin in range(0, pages, per_block):
            seen = visible[s * pages + begin : s * pages + begin + per_block]

            @pl.when(jnp.logical_not(every) & functools.reduce(jnp.logical_or, seen))
            def _():
                bias = jnp.zeros((1, length), jnp.float32)
                for i in range(per_block):
                    bias = jnp.where((lane == i) & jnp.logical_not(seen[i]), NEGATIVE, bias)
                items = items_of(shard, begin * page_len, length, bias)
                absorb(items, query, scale, acc, top, total)


def first_kernel(shards, heads, head_dim, page_len, scale, *refs):
    meta, queries, own, cosines, sines, mask = refs[:6]
    kv = refs[6 : 6 + shards]
    query, acc, top, total, cache = refs[6 + shards :]
    group_len = queries.shape[0]
    cos, sin = cosines[...], sines[...]
    keys_new = rotate(own[:, :head_dim].astype(jnp.float32), cos, sin).astype(jnp.bfloat16)
    cache[:, :head_dim] = keys_new
    cache[:, head_dim:] = own[:, head_dim:]
    for h in range(heads):
        vectors = queries[:, h * head_dim : (h + 1) * head_dim].astype(jnp.float32)
        query[pl.ds(h * group_len, group_len), :] = rotate(vectors, cos, sin).astype(jnp.bfloat16)
    acc[...] = jnp.zeros_like(acc)
    total[...] = jnp.zeros_like(total)
    top[...] = jnp.full(top.shape, NEGATIVE, jnp.float32)
    items = [
        (
            pl.ds(h * group_len, group_len),
            lambda: cache[:, :head_dim],
            lambda: cache[:, head_dim:],
            mask[...],
        )
        for h in range(heads)
    ]
    absorb(items, query, scale, acc, top, total)
    absorb_pages(kv, meta, page_len, query, scale, acc, top, total)


def rest_kernel(shards, heads, head_dim, page_len, scale, *refs):
    meta, query, acc_in, top_in, total_in, residual = refs[:6]
    kv = refs[6 : 6 + shards]
    stream, acc, top, total = refs[6 + shards :]
    group_len = residual.shape[0]
    acc[...] = acc_in[...]
    top[...] = top_in[...]
    total[...] = total_in[...]
    absorb_pages(kv, meta, page_len, query, scale, acc, top, total)
    for h in range(heads):
        at = pl.ds(h * group_len, group_len)
        lanes = slice(h * head_dim, (h + 1) * head_dim)
        attended = acc[at, :] / jnp.sum(total[at, :], 1, keepdims=True)
        stream[:, lanes] = (residual[:, lanes].astype(jnp.float32) + attended).astype(jnp.bfloat16)


def spread(vectors, lane):
    rows, depth = vectors.shape
    step = 128
    source = lax.broadcasted_iota(jnp.int32, (step, 2 * step), 0)
    target = lax.broadcasted_iota(jnp.int32, (step, 2 * step), 1)
    place = jnp.where(target == 2 * source + lane, 1.0, 0.0).astype(jnp.bfloat16)
    return [
        jnp.dot(vectors[:, k : k + step], place, preferred_element_type=jnp.float32).astype(
            jnp.bfloat16
        )
        for k in range(0, depth, step)
    ]


def lhs_kernel(parts, blocks, *refs):
    meta, gain = refs[:2]
    streams = refs[2 : 2 + parts]
    lhs, squares, held = refs[2 + parts :]
    per_part = blocks // parts if blocks > parts else 1
    block_len = held.shape[1]
    for j, stream in enumerate(streams):
        for i in range(per_part):
            held[meta[1 + j] * per_part + i] = stream[pl.ds(i * block_len, block_len), :]
    for p in range(blocks):
        vectors = held[lax.bitwise_xor(meta[0], blocks - 1 - p)].astype(jnp.float32)
        square = jnp.sum(vectors * vectors, 1, keepdims=True)
        squares[pl.ds(p, 1), :] = jnp.broadcast_to(square, (block_len, 128)).T[:1, :]
        scaled = (vectors * gain[...]).astype(jnp.bfloat16)
        for half in range(2):
            for i, piece in enumerate(spread(scaled, half)):
                lhs[half, p, :, i * 256 : (i + 1) * 256] = piece


def send_kernel(lhs, weights, out):
    product = times(lhs, weights)
    out[...] = product.astype(jnp.bfloat16).reshape(out.shape)


def keep_kernel(axis, lhs, weights, got, send, keep):
    product = times(lhs, weights).reshape(got.shape)
    summed = (product + got[...].astype(jnp.float32)).astype(jnp.bfloat16)
    high, low = send.shape[1], send.shape[2]
    summed = summed.reshape((2, high, 2, low) + got.shape[-2:])
    send[...] = summed[:, :, 0]
    keep[...] = summed[:, :, 1]


def times(lhs, weights):
    depth = lhs.shape[-1]
    return jnp.dot(
        lhs[...].reshape(-1, depth),
        weights[...].reshape(depth, weights.shape[-1]),
        preferred_element_type=jnp.float32,
    )


def vmem_call(kernel, n_in, out_shape, scratch, flops):
    whole = pl.BlockSpec(memory_space=pltpu.VMEM)
    return pl.pallas_call(
        kernel,
        in_specs=[pl.BlockSpec(memory_space=pltpu.SMEM)] + [whole] * n_in,
        out_specs=jax.tree.map(lambda _: whole, out_shape),
        out_shape=out_shape,
        scratch_shapes=scratch,
        compiler_params=pltpu.CompilerParams(vmem_limit_bytes=48 << 20),
        cost_estimate=pl.CostEstimate(flops=1, bytes_accessed=1, transcendentals=0),
    )


def gather_near(own, size, index):
    twin = [(r, r ^ 1) for r in range(size)]
    far = []
    for shift in range(1, size // 2):
        pairs = [(r, (r + 2 * shift) % size) for r in range(size)]
        far.append((lax.ppermute(own, "req", pairs), (index - 2 * shift) % size))
    return [(own, index), (lax.ppermute(own, "req", twin), index ^ 1)], far


def gather_far(far, size):
    twin = [(r, r ^ 1) for r in range(size)]
    return far + [(lax.ppermute(part, "req", twin), origin ^ 1) for part, origin in far]


def on_device(
    queries,
    suffix_key_value,
    residual,
    gain,
    gate_up,
    prefix_cache_slots,
    prefix_page_slots,
    lengths,
    counts,
):
    blocks = lax.axis_size("blk")
    groups = lax.axis_size("req")
    column = lax.axis_index("blk")
    group_index = lax.axis_index("req")
    group_len = queries.shape[0]
    heads_kv = suffix_key_value.shape[1]
    head_dim = suffix_key_value.shape[2] // 2
    heads_here = queries.shape[1] // head_dim
    slots_here, page_len = prefix_cache_slots.shape[:2]
    score_scale = math.log2(math.e) / math.sqrt(head_dim)
    kv_head = column * heads_kv // blocks
    page_count = counts[group_index]

    own_slots = lax.dynamic_index_in_dim(prefix_cache_slots, kv_head, 2, keepdims=False)
    own_slots = own_slots.reshape(slots_here * page_len, 2 * head_dim)
    near, far = gather_near(own_slots, groups, group_index)

    request, offset, positions = suffix_layout(
        lengths[group_index], page_count, group_len, page_len
    )
    cosines, sines = rope_tables(positions, head_dim // 2)
    own_head = lax.dynamic_index_in_dim(suffix_key_value, kv_head, 1, keepdims=False)
    allowed = (request[:, None] == request[None, :]) & (offset[None, :] <= offset[:, None])
    mask = jnp.where(allowed, 0.0, NEGATIVE).astype(jnp.float32)

    pages_total = prefix_page_slots.shape[0]
    page_ids = jnp.arange(pages_total, dtype=jnp.int32)
    match = prefix_page_slots[None, :] == page_ids[:, None]
    page_of_slot = jnp.sum(jnp.where(match, page_ids[None, :], 0), 1).reshape(groups, slots_here)

    def meta(parts):
        ids = [lax.dynamic_index_in_dim(page_of_slot, o, 0, keepdims=False) for _, o in parts]
        return jnp.concatenate([page_count[None]] + ids)

    rows = heads_here * group_len
    state = (
        jax.ShapeDtypeStruct((rows, head_dim), jnp.float32),
        jax.ShapeDtypeStruct((rows, head_dim), jnp.float32),
        jax.ShapeDtypeStruct((rows, head_dim), jnp.float32),
    )
    key_flops = 4 * rows * head_dim * slots_here * page_len
    query, acc, top, total, both_new = vmem_call(
        functools.partial(first_kernel, len(near), heads_here, head_dim, page_len, score_scale),
        5 + len(near),
        (jax.ShapeDtypeStruct((rows, head_dim), jnp.bfloat16),)
        + state
        + (jax.ShapeDtypeStruct((group_len, 2 * head_dim), jnp.bfloat16),),
        [],
        key_flops * len(near),
    )(meta(near), queries, own_head, cosines, sines, mask, *[part for part, _ in near])
    arrived = lax.optimization_barrier(([part for part, _ in far], top))[0]
    far = gather_far([(part, origin) for part, (_, origin) in zip(arrived, far)], groups)
    stream = vmem_call(
        functools.partial(rest_kernel, len(far), heads_here, head_dim, page_len, score_scale),
        5 + len(far),
        jax.ShapeDtypeStruct((group_len, heads_here * head_dim), jnp.bfloat16),
        [pltpu.VMEM((rows, head_dim), jnp.float32)] * 3,
        key_flops * len(far),
    )(meta(far), query, acc, top, total, residual, *[part for part, _ in far])

    lane_width = 2 * heads_kv * head_dim // blocks
    updated_cache = lax.dynamic_slice_in_dim(
        both_new, column * lane_width % (2 * head_dim), lane_width, 1
    )

    near, far = gather_near(stream, groups, group_index)
    streams = near + gather_far(far, groups)
    features = stream.shape[1]
    bits = blocks.bit_length() - 1
    block_len = groups * group_len // blocks
    lhs, squares = vmem_call(
        functools.partial(lhs_kernel, groups, blocks),
        1 + groups,
        (
            jax.ShapeDtypeStruct((2, blocks, block_len, 2 * features), jnp.bfloat16),
            jax.ShapeDtypeStruct((blocks, block_len), jnp.float32),
        ),
        [pltpu.VMEM((blocks, block_len, features), jnp.bfloat16)],
        8 * groups * group_len * features * 128,
    )(
        jnp.stack([column] + [origin for _, origin in streams]),
        gain[None, :],
        *[part for part, _ in streams],
    )

    def swap(array, bit):
        return lax.ppermute(array, "blk", [(b, b ^ (1 << bit)) for b in range(blocks)])

    def halves(array, bit, left, lead):
        low = sum(1 for other in left if other < bit)
        shape = array.shape[:lead] + (-1, 2, 1 << low) + array.shape[lead + 1 :]
        split = array.reshape(shape)
        out = array.shape[:lead] + (-1,) + array.shape[lead + 1 :]
        return [
            lax.index_in_dim(split, i, lead + 1, keepdims=False).reshape(out) for i in range(2)
        ]

    def add(keep, got):
        return (keep.astype(jnp.float32) + got.astype(jnp.float32)).astype(keep.dtype)

    def multiply(which, bit, begin, end, lhs, got=None, next_bit=None):
        width = end - begin
        tile = 128 * math.gcd(math.gcd(begin // 128, width // 128), 2)
        low = 1 << bit
        high = blocks // (2 * low)
        rows = lhs.reshape(2, high, 2, low, block_len, 2 * features)
        in_specs = [
            pl.BlockSpec(
                (2, high, None, low, block_len, 2 * features), lambda j: (0, 0, which, 0, 0, 0)
            ),
            pl.BlockSpec((features, 2, tile), lambda j: (0, 0, begin // tile + j)),
        ]
        operands = [rows, gate_up]
        if got is None:
            kernel = send_kernel
            out = (2, high * low, block_len, width)
            out_specs = pl.BlockSpec(out[:-1] + (tile,), lambda j: (0, 0, 0, j))
            out_shape = jax.ShapeDtypeStruct(out, jnp.bfloat16)
        else:
            rest = [other for other in range(bits) if other != bit]
            next_low = 1 << sum(1 for other in rest if other < next_bit)
            next_high = high * low // (2 * next_low)
            out = (2, next_high, next_low, block_len, width)
            spec = pl.BlockSpec(out[:-1] + (tile,), lambda j: (0, 0, 0, 0, j))
            kernel = functools.partial(keep_kernel, None)
            in_specs.append(
                pl.BlockSpec((2, high * low, block_len, tile), lambda j: (0, 0, 0, j))
            )
            operands.append(got)
            out_specs = (spec, spec)
            out_shape = (jax.ShapeDtypeStruct(out, jnp.bfloat16),) * 2
        result = pl.pallas_call(
            kernel,
            grid=(width // tile,),
            in_specs=in_specs,
            out_specs=out_specs,
            out_shape=out_shape,
            compiler_params=pltpu.CompilerParams(vmem_limit_bytes=48 << 20),
            cost_estimate=pl.CostEstimate(flops=1, bytes_accessed=1, transcendentals=0),
        )(*operands)
        if got is None:
            return result
        return [part.reshape((2, -1, block_len, width)) for part in result]

    width_here = gate_up.shape[2]
    units = width_here // 128
    whole_units = sum(size for size, _ in CHUNKS)
    bounds, so_far = [0], 0
    for size, _ in CHUNKS:
        so_far += size
        bounds.append(128 * max(bounds[-1] // 128 + 1, units * so_far // whole_units))
    orders = [list(order) + list(range(len(order), bits)) for _, order in CHUNKS]

    pieces = [None] * len(CHUNKS)
    flying, kept, lefts = {}, {}, {}
    square_sum, square_keep, square_left = squares, None, list(range(bits))
    token = squares

    def after(array):
        return lax.optimization_barrier((array, token))[0]

    for step in STEPS:
        kind, c = step[0], int(step[1:])
        if kind == "Q":
            if c == 0:
                square_sum = after(squares)
            else:
                square_sum = add(after(square_keep), flying["Q"])
                square_left.remove(c - 1)
            for bit in [c] if c < 2 else range(c, bits):
                if bit > c:
                    square_sum = add(square_keep, flying["Q"])
                    square_left.remove(bit - 1)
                send, square_keep = halves(square_sum, bit, square_left, 0)
                flying["Q"] = swap(send, bit)
            token = square_sum
            continue
        begin, end, order = bounds[c], bounds[c + 1], orders[c]
        if kind == "S":
            send = multiply(0, order[0], begin, end, after(lhs))
            lefts[c] = list(range(bits))
            flying[c] = swap(send, order[0])
            token = send
        elif kind == "K":
            send, kept[c] = multiply(1, order[0], begin, end, lhs, after(flying[c]), order[1])
            lefts[c].remove(order[0])
            flying[c] = swap(send, order[1])
            token = send
        elif kind == "A":
            for n in range(2, bits):
                summed = add(after(kept[c]), flying[c])
                lefts[c].remove(order[n - 1])
                send, kept[c] = halves(summed, order[n], lefts[c], 1)
                flying[c] = swap(send, order[n])
            token = send
        else:
            summed = after(kept[c]).astype(jnp.float32) + flying[c].astype(jnp.float32)
            norm = lax.rsqrt(
                (square_keep + flying["Q"]).reshape(block_len, 1) / D + EPSILON
            )
            summed = summed.reshape(2, block_len, end - begin) * norm
            pieces[c] = (jax.nn.silu(summed[0]) * summed[1]).astype(jnp.bfloat16)
            token = pieces[c]
    return (jnp.concatenate(pieces, 1), updated_cache)


def solution(mesh):
    placed = (
        P("req", "blk"),
        P("req", None, None),
        P("req", "blk"),
        P("blk"),
        P("blk", None, "req"),
        P("req", None, None, None),
        P(),
        P(),
        P(),
    )
    return jax.shard_map(
        on_device,
        mesh=mesh,
        in_specs=placed,
        out_specs=(P("blk", "req"), P("req", "blk")),
        check_vma=False,
    )
```

time: 252 us -> 138 us (0.55)
  waiting for transfers between devices: 151 us -> 30.9 us
  Pallas kernels: 0 us -> 57.7 us
  starting transfers between devices: 0.3 us -> 37.8 us
  matrix products: 24.1 us -> 0 us
  blocking collectives: 21.4 us -> 0 us
  local copies, waits for them, and re-layouts: 26.5 us -> 5.53 us
  between operations: 14.7 us -> 1.83 us
  other arithmetic: 14.2 us -> 3.74 us
    reduce_scatter x1 -> x0, waiting for transfers between devices: 129 us -> none  [on_device(): lax.psum_scatter(jnp.dot(gathered, weights, preferred_element_type=jnp.fl...]
    pallas_call x0 -> x15, Pallas kernels: none -> 57.7 us  [the longest x12 40.4 us: multiply(): pl.pallas_call(kernel, grid=(width // tile,), in_specs=in_specs, out_spec...]
    ppermute x0 -> x27, starting transfers between devices: none -> 37.8 us  [the longest x21 32.9 us: swap(): lax.ppermute(array, 'blk', [(b, b ^ 1 << bit) for b in range(blocks)])]
    ppermute x0 -> x27, waiting for transfers between devices: none -> 30.9 us  [the longest x21 21.1 us: swap(): lax.ppermute(array, 'blk', [(b, b ^ 1 << bit) for b in range(blocks)])]
    dot_general x11 -> x0, matrix products: 24.1 us -> none  [the longest x1 13.2 us: on_device(): jnp.dot(gathered, weights, preferred_element_type=jnp.float32)]
    psum x1 -> x0, blocking collectives: 21.4 us -> none  [on_device(): square_sum = lax.psum(jnp.sum(stream_f32 * stream_f32, 1), 'blk')]
    all_gather x2 -> x0, waiting for transfers between devices: 21.1 us -> none  [the longest x1 21.1 us: on_device(): shard_piece = lax.all_gather(own_slots, 'req', axis=0, tiled=True)]
    unnamed x21 -> x18, local copies, waits for them, and re-layouts: 17.5 us -> 0.9 us
  transfers between devices with their start and end apart: 3 -> 27, of which waited for: 2 -> 14; matrix products, arithmetic and copies ran while one was open for 8% -> 4% of each run, Pallas kernels for 0% -> 33%
where the time goes in v1:
time: 138 us; the launch traced here: 137 us
  Pallas kernels  57.7 us (42%)
  starting transfers between devices  37.8 us (27%)
  waiting for transfers between devices  30.9 us (22%)
  local copies, waits for them, and re-layouts  5.53 us (4%)
  other arithmetic  3.74 us (3%)
  between operations  1.83 us (1%)
    pallas_call x12, Pallas kernels, multiply(): pl.pallas_call(kernel, grid=(width // tile,), in_specs=in_specs, out_spec...  40.4 us
    ppermute x21, starting transfers between devices, swap(): lax.ppermute(array, 'blk', [(b, b ^ 1 << bit) for b in range(blocks)])  32.9 us
    ppermute x21, waiting for transfers between devices, swap(): lax.ppermute(array, 'blk', [(b, b ^ 1 << bit) for b in range(blocks)])  21.1 us
    pallas_call x1, Pallas kernels, on_device(): vmem_call(functools.partial(first_kernel, len(near), heads_here, head_dim...  8.66 us
    ppermute x2, waiting for transfers between devices, gather_near(): far.append((lax.ppermute(own, 'req', pairs), (index - 2 * shift) % size))  7.09 us
    pallas_call x1, Pallas kernels, on_device(): vmem_call(functools.partial(rest_kernel, len(far), heads_here, head_dim,...  6.73 us
    ppermute x2, starting transfers between devices, gather_near(): far.append((lax.ppermute(own, 'req', pairs), (index - 2 * shift) % size))  4.42 us
    dynamic_slice x1, local copies, waits for them, and re-layouts, on_device(): lax.dynamic_index_in_dim(prefix_cache_slots, kv_head, 2, keepdims=False)  3.35 us
  transfers between devices with their start and end apart: 27, of which 14 were waited for; matrix products, arithmetic and copies ran while one was open for 4% of the time, Pallas kernels for 33%

profile of v1, /device:TPU:0, one launch (start us, length us, event | category | flops | bytes accessed | tf_op | source)
XLA Modules:
  0.0 137.5 jit_solution(5399415808200457845)
XLA Ops:
  0.7 3.3 %constant_dynamic-slice_fusion = bf16[8,128,1,256]{3,2,1,0:T(2,128)(2,1)S(1)} fusion(bf16[8,128,8,256]{3,2,1,0:T(8,128)(2,1)} %param.14, s32[]{:T(128)S(6)} %select_n.56), kind=kLoop, calls=%fused_computation.79 | loop fusion | bytes 1048580 | tf_op jit(solution)/shard_map/jit(dynamic_index_in_dim)/dynamic_slice | solution.py:272
  4.2 0.5 collective-permute-start
  4.7 2.6 %collective-permute-start.1 = (bf16[1024,256]{1,0:T(8,128)(2,1)S(1)}, bf16[1024,256]{1,0:T(8,128)(2,1)S(1)}, u32[]{:S(2)}, u32[]{:S(2)}) collective-permute-start(bf16[1024,256]{1,0:T(8,128)(2,1)S(1)} %bitcast.217), channel_id=1, source_target_pairs={{0,16},{8,24},{16,0},{24,8},{1,17},{9,25},{17,1},{25,9},{2,18},{10... | collective-permute-start | bytes 1572872 | tf_op jit(solution)/shard_map/ppermute | solution.py:239
  7.3 0.1 constant_dynamic-slice_fusion.2
  7.5 0.1 select_reduce_fusion
  7.7 0.7 dynamic_slice.28
  8.3 0.2 reduce-window_clone.1
  9.4 0.7 pad_add_fusion.1.refs_0_
  10.1 0.3 fusion.19
  10.4 0.1 pad_maximum_fusion
  10.5 0.1 and_select_fusion.refs_5_
  10.6 8.7 %shard_map.104 = (bf16[1024,128]{1,0:T(8,128)(2,1)S(1)}, f32[1024,128]{1,0:T(8,128)S(1)}, f32[1024,128]{1,0:T(8,128)S(1)}, f32[1024,128]{1,0:T(8,128)S(1)}, bf16[128,256]{1,0:T(8,128)(2,1)}) custom-call(s32[17]{0:T(128)S(1)} %pad_add_fusion.1.refs_0_, bf16[128,1024]{1,0:T(8,128)(2,1)S(1)} %copy-done.2, bf16[128,256]{1,0:T(8,128)(2,1)S(1)} %bitcast.221, ...), custom_call_target="tpu_custom_call" | custom-call | flops 1 | bytes 1 | tf_op jit(solution)/shard_map/pallas_call | solution.py:300
  19.3 0.5 collective-permute-done.1.refs_6_
  19.8 0.7 pad_add_fusion.refs_0_
  20.5 1.2 collective-permute-done.2.refs_7_
  21.7 6.7 %shard_map.105.refs_2_ = bf16[128,1024]{1,0:T(8,128)(2,1)S(1)} custom-call(s32[17]{0:T(128)S(1)} %pad_add_fusion.refs_0_, bf16[1024,128]{1,0:T(8,128)(2,1)S(1)} %get-tuple-element.49.refs_1_, f32[1024,128]{1,0:T(8,128)S(1)} %get-tuple-element.50.refs_2_, f32[1024,128]{1,0:T(8,128)S(1)} %get-tuple-element.51.refs_3_, ...), custom_call_target="tpu_custom_call" | custom-call | flops 1 | bytes 1 | tf_op jit(solution)/shard_map/pallas_call | solution.py:311
  28.5 1.8 %collective-permute-start.4 = (bf16[128,1024]{1,0:T(8,128)(2,1)S(1)}, bf16[128,1024]{1,0:T(8,128)(2,1)S(1)}, u32[]{:S(2)}, u32[]{:S(2)}) collective-permute-start(bf16[128,1024]{1,0:T(8,128)(2,1)S(1)} %shard_map.105.refs_2_), channel_id=1, source_target_pairs={{0,16},{8,24},{16,0},{24,8},{1,17},{9,25},{17,1},{25,9},{2,18},{10... | collective-permute-start | bytes 786440 | tf_op jit(solution)/shard_map/ppermute | solution.py:239
  30.3 6.6 %collective-permute-done.4.refs_4_ = bf16[128,1024]{1,0:T(8,128)(2,1)S(1)} collective-permute-done((bf16[128,1024]{1,0:T(8,128)(2,1)S(1)}, bf16[128,1024]{1,0:T(8,128)(2,1)S(1)}, u32[]{:S(2)}, u32[]{:S(2)}) %collective-permute-start.4) | collective-permute-done | bytes 262176 | tf_op jit(solution)/shard_map/ppermute | solution.py:239
  37.0 1.4 %collective-permute-done.5.refs_5_ = bf16[128,1024]{1,0:T(8,128)(2,1)S(1)} collective-permute-done((bf16[128,1024]{1,0:T(8,128)(2,1)S(1)}, bf16[128,1024]{1,0:T(8,128)(2,1)S(1)}, u32[]{:S(2)}, u32[]{:S(2)}) %collective-permute-start.5) | collective-permute-done | bytes 262176 | tf_op jit(solution)/shard_map/ppermute | solution.py:245
  38.4 1.9 %shard_map.106 = (bf16[2,8,64,2048]{3,2,1,0:T(8,128)(2,1)S(1)}, f32[8,64]{1,0:T(8,128)S(1)}) custom-call(s32[5]{0:T(128)S(1)} %stack.23.refs_0_, f32[1,1024]{1,0:T(1,128)S(1)} %bitcast.223, bf16[128,1024]{1,0:T(8,128)(2,1)S(1)} %shard_map.105.refs_2_, bf16[128,1024]{1,0:T(8,128)(2,1)S(1)} %collective-permute-done.3.refs_3_, ...), custom_call_target="tpu_custom_call" | custom-call | flops 1 | bytes 1 | tf_op jit(solution)/shard_map/pallas_call | solution.py:329
  40.3 4.3 %shard_map.107 = bf16[2,4,64,768]{3,2,1,0:T(8,128)(2,1)S(1)} custom-call(bf16[2,4,2,1,64,2048]{5,4,3,2,1,0:T(8,128)(2,1)S(1)} %bitcast.204, bf16[1024,2,3584]{2,1,0:T(2,128)(2,1)} %weights.23), custom_call_target="tpu_custom_call" | custom-call | flops 1 | bytes 1 | tf_op jit(solution)/shard_map/pallas_call | solution.py:390
  44.6 1.8 %collective-permute-start.6 = (bf16[2,4,64,768]{3,2,1,0:T(8,128)(2,1)S(1)}, bf16[2,4,64,768]{3,2,1,0:T(8,128)(2,1)S(1)}, u32[]{:S(2)}, u32[]{:S(2)}) collective-permute-start(bf16[2,4,64,768]{3,2,1,0:T(8,128)(2,1)S(1)} %shard_map.107), channel_id=1, source_target_pairs={{0,1},{1,0},{2,3},{3,2},{4,5},{5,4},{6,7},{7,6},{8,9},{9,8},{10,11... | collective-permute-start | bytes 2359304 | tf_op jit(solution)/shard_map/ppermute | solution.py:345
  46.4 4.0 %shard_map.108 = bf16[2,4,64,768]{3,2,1,0:T(8,128)(2,1)S(1)} custom-call(bf16[2,2,2,2,64,2048]{5,4,3,2,1,0:T(8,128)(2,1)S(1)} %bitcast.205, bf16[1024,2,3584]{2,1,0:T(2,128)(2,1)} %weights.23), custom_call_target="tpu_custom_call" | custom-call | flops 1 | bytes 1 | tf_op jit(solution)/shard_map/pallas_call | solution.py:390
  50.4 1.6 %collective-permute-start.10 = (bf16[2,4,64,768]{3,2,1,0:T(8,128)(2,1)S(1)}, bf16[2,4,64,768]{3,2,1,0:T(8,128)(2,1)S(1)}, u32[]{:S(2)}, u32[]{:S(2)}) collective-permute-start(bf16[2,4,64,768]{3,2,1,0:T(8,128)(2,1)S(1)} %shard_map.108), channel_id=1, source_target_pairs={{0,2},{1,3},{2,0},{3,1},{4,6},{5,7},{6,4},{7,5},{8,10},{9,11},{10,... | collective-permute-start | bytes 2359304 | tf_op jit(solution)/shard_map/ppermute | solution.py:345
  52.1 4.0 %shard_map.109 = bf16[2,4,64,768]{3,2,1,0:T(8,128)(2,1)S(1)} custom-call(bf16[2,4,2,1,64,2048]{5,4,3,2,1,0:T(8,128)(2,1)S(1)} %bitcast.206, bf16[1024,2,3584]{2,1,0:T(2,128)(2,1)} %weights.23), custom_call_target="tpu_custom_call" | custom-call | flops 1 | bytes 1 | tf_op jit(solution)/shard_map/pallas_call | solution.py:390
  56.1 0.6 collective-permute-start.9
  56.7 2.8 %shard_map.110 = bf16[2,4,64,512]{3,2,1,0:T(8,128)(2,1)S(1)} custom-call(bf16[2,2,2,2,64,2048]{5,4,3,2,1,0:T(8,128)(2,1)S(1)} %bitcast.207, bf16[1024,2,3584]{2,1,0:T(2,128)(2,1)} %weights.23), custom_call_target="tpu_custom_call" | custom-call | flops 1 | bytes 1 | tf_op jit(solution)/shard_map/pallas_call | solution.py:390
  59.6 0.3 collective-permute-start.8
  59.9 2.8 %shard_map.111 = bf16[2,4,64,512]{3,2,1,0:T(8,128)(2,1)S(1)} custom-call(bf16[2,4,2,1,64,2048]{5,4,3,2,1,0:T(8,128)(2,1)S(1)} %bitcast.208, bf16[1024,2,3584]{2,1,0:T(2,128)(2,1)} %weights.23), custom_call_target="tpu_custom_call" | custom-call | flops 1 | bytes 1 | tf_op jit(solution)/shard_map/pallas_call | solution.py:390
  62.7 1.8 %collective-permute-start.7 = (bf16[2,4,64,512]{3,2,1,0:T(8,128)(2,1)S(1)}, bf16[2,4,64,512]{3,2,1,0:T(8,128)(2,1)S(1)}, u32[]{:S(2)}, u32[]{:S(2)}) collective-permute-start(bf16[2,4,64,512]{3,2,1,0:T(8,128)(2,1)S(1)} %shard_map.111), channel_id=1, source_target_pairs={{0,1},{1,0},{2,3},{3,2},{4,5},{5,4},{6,7},{7,6},{8,9},{9,8},{10,11... | collective-permute-start | bytes 1572872 | tf_op jit(solution)/shard_map/ppermute | solution.py:345
  64.5 0.6 collective-permute-done.6.got
  65.1 4.1 %shard_map.112 = (bf16[2,1,2,64,768]{4,3,2,1,0:T(8,128)(2,1)S(1)}, bf16[2,1,2,64,768]{4,3,2,1,0:T(8,128)(2,1)S(1)}) custom-call(bf16[2,4,2,1,64,2048]{5,4,3,2,1,0:T(8,128)(2,1)S(1)} %bitcast.209, bf16[1024,2,3584]{2,1,0:T(2,128)(2,1)} %weights.23, bf16[2,4,64,768]{3,2,1,0:T(8,128)(2,1)S(1)} %collective-permute-done.6.got), custom_call_target="tpu_custom_call" | custom-call | flops 1 | bytes 1 | tf_op jit(solution)/shard_map/pallas_call | solution.py:390
  69.2 2.9 %collective-permute-start.11 = (bf16[2,2,64,768]{3,2,0,1:T(8,128)(2,1)S(1)}, bf16[2,2,64,768]{3,2,0,1:T(8,128)(2,1)S(1)}, u32[]{:S(2)}, u32[]{:S(2)}) collective-permute-start(bf16[2,2,64,768]{3,2,0,1:T(8,128)(2,1)S(1)} %bitcast.232), channel_id=1, source_target_pairs={{0,4},{1,5},{2,6},{3,7},{4,0},{5,1},{6,2},{7,3},{8,12},{9,13},{10,... | collective-permute-start | bytes 1179656 | tf_op jit(solution)/shard_map/ppermute | solution.py:345
  72.1 4.1 %shard_map.113 = (bf16[2,2,1,64,768]{4,3,2,1,0:T(8,128)(2,1)S(1)}, bf16[2,2,1,64,768]{4,3,2,1,0:T(8,128)(2,1)S(1)}) custom-call(bf16[2,2,2,2,64,2048]{5,4,3,2,1,0:T(8,128)(2,1)S(1)} %bitcast.210, bf16[1024,2,3584]{2,1,0:T(2,128)(2,1)} %weights.23, bf16[2,4,64,768]{3,2,1,0:T(8,128)(2,1)S(1)} %collective-permute-done.10.got), custom_call_target="tpu_custom_call" | custom-call | flops 1 | bytes 1 | tf_op jit(solution)/shard_map/pallas_call | solution.py:390
  76.2 1.6 %collective-permute-start.13 = (bf16[2,2,64,768]{3,2,0,1:T(8,128)(2,1)S(1)}, bf16[2,2,64,768]{3,2,0,1:T(8,128)(2,1)S(1)}, u32[]{:S(2)}, u32[]{:S(2)}) collective-permute-start(bf16[2,2,64,768]{3,2,0,1:T(8,128)(2,1)S(1)} %bitcast.231), channel_id=1, source_target_pairs={{0,1},{1,0},{2,3},{3,2},{4,5},{5,4},{6,7},{7,6},{8,9},{9,8},{10,11... | collective-permute-start | bytes 1179656 | tf_op jit(solution)/shard_map/ppermute | solution.py:345
  77.7 2.1 %shard_map.114 = bf16[2,4,64,256]{3,2,1,0:T(8,128)(2,1)S(1)} custom-call(bf16[2,2,2,2,64,2048]{5,4,3,2,1,0:T(8,128)(2,1)S(1)} %bitcast.211, bf16[1024,2,3584]{2,1,0:T(2,128)(2,1)} %weights.23), custom_call_target="tpu_custom_call" | custom-call | flops 1 | bytes 1 | tf_op jit(solution)/shard_map/pallas_call | solution.py:390
  79.8 2.1 %collective-permute-done.9.got = bf16[2,4,64,768]{3,2,1,0:T(8,128)(2,1)S(1)} collective-permute-done((bf16[2,4,64,768]{3,2,1,0:T(8,128)(2,1)S(1)}, bf16[2,4,64,768]{3,2,1,0:T(8,128)(2,1)S(1)}, u32[]{:S(2)}, u32[]{:S(2)}) %collective-permute-start.9) | collective-permute-done | bytes 786464 | tf_op jit(solution)/shard_map/ppermute | solution.py:345
  81.9 1.8 %collective-permute-start.12 = (bf16[2,4,64,256]{3,2,1,0:T(8,128)(2,1)S(1)}, bf16[2,4,64,256]{3,2,1,0:T(8,128)(2,1)S(1)}, u32[]{:S(2)}, u32[]{:S(2)}) collective-permute-start(bf16[2,4,64,256]{3,2,1,0:T(8,128)(2,1)S(1)} %shard_map.114), channel_id=1, source_target_pairs={{0,2},{1,3},{2,0},{3,1},{4,6},{5,7},{6,4},{7,5},{8,10},{9,11},{10,... | collective-permute-start | bytes 786440 | tf_op jit(solution)/shard_map/ppermute | solution.py:345
  83.7 4.1 %shard_map.115 = (bf16[2,1,2,64,768]{4,3,2,1,0:T(8,128)(2,1)S(1)}, bf16[2,1,2,64,768]{4,3,2,1,0:T(8,128)(2,1)S(1)}) custom-call(bf16[2,4,2,1,64,2048]{5,4,3,2,1,0:T(8,128)(2,1)S(1)} %bitcast.212, bf16[1024,2,3584]{2,1,0:T(2,128)(2,1)} %weights.23, bf16[2,4,64,768]{3,2,1,0:T(8,128)(2,1)S(1)} %collective-permute-done.9.got), custom_call_target="tpu_custom_call" | custom-call | flops 1 | bytes 1 | tf_op jit(solution)/shard_map/pallas_call | solution.py:390
  87.8 2.8 %collective-permute-done.8.got = bf16[2,4,64,512]{3,2,1,0:T(8,128)(2,1)S(1)} collective-permute-done((bf16[2,4,64,512]{3,2,1,0:T(8,128)(2,1)S(1)}, bf16[2,4,64,512]{3,2,1,0:T(8,128)(2,1)S(1)}, u32[]{:S(2)}, u32[]{:S(2)}) %collective-permute-start.8) | collective-permute-done | bytes 524320 | tf_op jit(solution)/shard_map/ppermute | solution.py:345
  90.6 1.7 %collective-permute-start.14 = (bf16[2,2,64,768]{3,2,1,0:T(8,128)(2,1)S(1)}, bf16[2,2,64,768]{3,2,1,0:T(8,128)(2,1)S(1)}, u32[]{:S(2)}, u32[]{:S(2)}) collective-permute-start(bf16[2,2,64,768]{3,2,1,0:T(8,128)(2,1)S(1)} %bitcast.225), channel_id=1, source_target_pairs={{0,4},{1,5},{2,6},{3,7},{4,0},{5,1},{6,2},{7,3},{8,12},{9,13},{10,... | collective-permute-start | bytes 1179656 | tf_op jit(solution)/shard_map/ppermute | solution.py:345
  92.3 2.8 %shard_map.116 = (bf16[2,2,1,64,512]{4,3,2,1,0:T(8,128)(2,1)S(1)}, bf16[2,2,1,64,512]{4,3,2,1,0:T(8,128)(2,1)S(1)}) custom-call(bf16[2,2,2,2,64,2048]{5,4,3,2,1,0:T(8,128)(2,1)S(1)} %bitcast.213, bf16[1024,2,3584]{2,1,0:T(2,128)(2,1)} %weights.23, bf16[2,4,64,512]{3,2,1,0:T(8,128)(2,1)S(1)} %collective-permute-done.8.got), custom_call_target="tpu_custom_call" | custom-call | flops 1 | bytes 1 | tf_op jit(solution)/shard_map/pallas_call | solution.py:390
  95.2 0.6 collective-permute-start.15
  95.8 3.1 %shard_map.117 = (bf16[2,2,1,64,512]{4,3,2,1,0:T(8,128)(2,1)S(1)}, bf16[2,2,1,64,512]{4,3,2,1,0:T(8,128)(2,1)S(1)}) custom-call(bf16[2,4,2,1,64,2048]{5,4,3,2,1,0:T(8,128)(2,1)S(1)} %bitcast.214, bf16[1024,2,3584]{2,1,0:T(2,128)(2,1)} %weights.23, bf16[2,4,64,512]{3,2,1,0:T(8,128)(2,1)S(1)} %collective-permute-done.7.got), custom_call_target="tpu_custom_call" | custom-call | flops 1 | bytes 1 | tf_op jit(solution)/shard_map/pallas_call | solution.py:390
  99.0 2.5 %collective-permute-start.17 = (bf16[2,2,64,512]{3,2,1,0:T(8,128)(2,1)S(1)}, bf16[2,2,64,512]{3,2,1,0:T(8,128)(2,1)S(1)}, u32[]{:S(2)}, u32[]{:S(2)}) collective-permute-start(bf16[2,2,64,512]{3,2,1,0:T(8,128)(2,1)S(1)} %bitcast.226), channel_id=1, source_target_pairs={{0,2},{1,3},{2,0},{3,1},{4,6},{5,7},{6,4},{7,5},{8,10},{9,11},{10,... | collective-permute-start | bytes 786440 | tf_op jit(solution)/shard_map/ppermute | solution.py:345
  101.7 1.7 %collective-permute-start.20 = (bf16[2,1,64,768]{3,2,0,1:T(8,128)(2,1)S(1)}, bf16[2,1,64,768]{3,2,0,1:T(8,128)(2,1)S(1)}, u32[]{:S(2)}, u32[]{:S(2)}) collective-permute-start(bf16[2,1,64,768]{3,2,0,1:T(8,128)(2,1)S(1)} %get-tuple-element.110), channel_id=1, source_target_pairs={{0,2},{1,3},{2,0},{3,1},{4,6},{5,7},{6,4},{7,5},{8,10},{9,11},{10,... | collective-permute-start | bytes 589832 | tf_op jit(solution)/shard_map/ppermute | solution.py:345
  103.5 2.1 %shard_map.118 = (bf16[2,2,1,64,256]{4,3,2,1,0:T(8,128)(2,1)S(1)}, bf16[2,2,1,64,256]{4,3,2,1,0:T(8,128)(2,1)S(1)}) custom-call(bf16[2,2,2,2,64,2048]{5,4,3,2,1,0:T(8,128)(2,1)S(1)} %bitcast.215, bf16[1024,2,3584]{2,1,0:T(2,128)(2,1)} %weights.23, bf16[2,4,64,256]{3,2,1,0:T(8,128)(2,1)S(1)} %collective-permute-done.12.got), custom_call_target="tpu_custom_call" | custom-call | flops 1 | bytes 1 | tf_op jit(solution)/shard_map/pallas_call | solution.py:390
  105.7 1.6 %collective-permute-start.18 = (bf16[2,2,64,256]{3,2,1,0:T(8,128)(2,1)S(1)}, bf16[2,2,64,256]{3,2,1,0:T(8,128)(2,1)S(1)}, u32[]{:S(2)}, u32[]{:S(2)}) collective-permute-start(bf16[2,2,64,256]{3,2,1,0:T(8,128)(2,1)S(1)} %bitcast.227), channel_id=1, source_target_pairs={{0,1},{1,0},{2,3},{3,2},{4,5},{5,4},{6,7},{7,6},{8,9},{9,8},{10,11... | collective-permute-start | bytes 393224 | tf_op jit(solution)/shard_map/ppermute | solution.py:345
  107.2 2.1 %collective-permute-done.14 = bf16[2,2,64,768]{3,2,1,0:T(8,128)(2,1)S(1)} collective-permute-done((bf16[2,2,64,768]{3,2,1,0:T(8,128)(2,1)S(1)}, bf16[2,2,64,768]{3,2,1,0:T(8,128)(2,1)S(1)}, u32[]{:S(2)}, u32[]{:S(2)}) %collective-permute-start.14) | collective-permute-done | bytes 393248 | tf_op jit(solution)/shard_map/ppermute | solution.py:345
  109.3 0.5 collective-permute-start.22
  110.0 0.6 collective-permute-start.16
  110.7 2.9 %collective-permute-done.16 = f32[4,64]{1,0:T(4,128)S(1)} collective-permute-done((f32[4,64]{1,0:T(4,128)S(1)}, f32[4,64]{1,0:T(4,128)S(1)}, u32[]{:S(2)}, u32[]{:S(2)}) %collective-permute-start.16) | collective-permute-done | bytes 1056 | tf_op jit(solution)/shard_map/ppermute | solution.py:345
  113.8 3.4 %collective-permute-start.19 = (f32[2,64]{1,0:T(2,128)S(1)}, f32[2,64]{1,0:T(2,128)S(1)}, u32[]{:S(2)}, u32[]{:S(2)}) collective-permute-start(f32[2,64]{1,0:T(2,128)S(1)} %bitcast.240), channel_id=1, source_target_pairs={{0,2},{1,3},{2,0},{3,1},{4,6},{5,7},{6,4},{7,5},{8,10},{9,11},{10,... | collective-permute-start | bytes 1544 | tf_op jit(solution)/shard_map/ppermute | solution.py:345
  117.2 1.5 %collective-permute-done.19 = f32[2,64]{1,0:T(2,128)S(1)} collective-permute-done((f32[2,64]{1,0:T(2,128)S(1)}, f32[2,64]{1,0:T(2,128)S(1)}, u32[]{:S(2)}, u32[]{:S(2)}) %collective-permute-start.19) | collective-permute-done | bytes 544 | tf_op jit(solution)/shard_map/ppermute | solution.py:345
  118.7 1.9 %collective-permute-start.21 = (f32[1,64]{1,0:T(1,128)S(1)}, f32[1,64]{1,0:T(1,128)S(1)}, u32[]{:S(2)}, u32[]{:S(2)}) collective-permute-start(f32[1,64]{1,0:T(1,128)S(1)} %slice_bitcast_fusion.24), channel_id=1, source_target_pairs={{0,4},{1,5},{2,6},{3,7},{4,0},{5,1},{6,2},{7,3},{8,12},{9,13},{10,... | collective-permute-start | bytes 776 | tf_op jit(solution)/shard_map/ppermute | solution.py:345
  120.6 2.1 %collective-permute-start.23 = (bf16[2,1,64,768]{3,2,0,1:T(8,128)(2,1)S(1)}, bf16[2,1,64,768]{3,2,0,1:T(8,128)(2,1)S(1)}, u32[]{:S(2)}, u32[]{:S(2)}) collective-permute-start(bf16[2,1,64,768]{3,2,0,1:T(8,128)(2,1)S(1)} %get-tuple-element.106), channel_id=1, source_target_pairs={{0,2},{1,3},{2,0},{3,1},{4,6},{5,7},{6,4},{7,5},{8,10},{9,11},{10,... | collective-permute-start | bytes 589832 | tf_op jit(solution)/shard_map/ppermute | solution.py:345
  122.7 0.9 collective-permute-start.24
  123.6 2.0 %collective-permute-start.25 = (bf16[2,1,64,512]{3,2,0,1:T(8,128)(2,1)S(1)}, bf16[2,1,64,512]{3,2,0,1:T(8,128)(2,1)S(1)}, u32[]{:S(2)}, u32[]{:S(2)}) collective-permute-start(bf16[2,1,64,512]{3,2,0,1:T(8,128)(2,1)S(1)} %get-tuple-element.112), channel_id=1, source_target_pairs={{0,4},{1,5},{2,6},{3,7},{4,0},{5,1},{6,2},{7,3},{8,12},{9,13},{10,... | collective-permute-start | bytes 393224 | tf_op jit(solution)/shard_map/ppermute | solution.py:345
  125.6 1.0 collective-permute-start.26
  127.0 2.1 %collective-permute-done.23 = bf16[2,1,64,768]{3,2,0,1:T(8,128)(2,1)S(1)} collective-permute-done((bf16[2,1,64,768]{3,2,0,1:T(8,128)(2,1)S(1)}, bf16[2,1,64,768]{3,2,0,1:T(8,128)(2,1)S(1)}, u32[]{:S(2)}, u32[]{:S(2)}) %collective-permute-start.23) | collective-permute-done | bytes 196640 | tf_op jit(solution)/shard_map/ppermute | solution.py:345
  129.2 5.2 %collective-permute-done.24 = bf16[2,1,64,512]{3,2,0,1:T(8,128)(2,1)S(1)} collective-permute-done((bf16[2,1,64,512]{3,2,0,1:T(8,128)(2,1)S(1)}, bf16[2,1,64,512]{3,2,0,1:T(8,128)(2,1)S(1)}, u32[]{:S(2)}, u32[]{:S(2)}) %collective-permute-start.24) | collective-permute-done | bytes 131104 | tf_op jit(solution)/shard_map/ppermute | solution.py:345
  134.6 1.3 collective-permute-done.25
  136.0 0.6 collective-permute-done.26
  136.7 0.8 copy-done.4
  (79 shorter events, 2.2 us)
Async XLA Ops:
  0.6 6.7 %copy-start = (bf16[128,8,256]{2,1,0:T(8,128)(2,1)S(1)}, bf16[128,8,256]{2,1,0:T(8,128)(2,1)}, u32[]{:S(2)}) copy-start(bf16[128,8,256]{2,1,0:T(8,128)(2,1)} %param.10) | copy-start | bytes 1572868
  0.6 6.8 %copy-start.6 = (s32[32]{0:T(128)S(1)}, s32[32]{0:T(128)}, u32[]{:S(2)}) copy-start(s32[32]{0:T(128)} %param.15) | copy-start | bytes 388
  0.7 7.0 %copy-start.7 = (s32[4]{0:T(128)S(1)}, s32[4]{0:T(128)}, u32[]{:S(2)}) copy-start(s32[4]{0:T(128)} %param.17) | copy-start | bytes 52
  0.7 7.7 %copy-start.5 = (s32[4,4]{1,0:T(4,128)S(1)}, s32[4,4]{1,0:T(4,128)}, u32[]{:S(2)}) copy-start(s32[4,4]{1,0:T(4,128)} %param.16) | copy-start | bytes 196
  0.7 10.0 %copy-start.2 = (bf16[128,1024]{1,0:T(8,128)(2,1)S(1)}, bf16[128,1024]{1,0:T(8,128)(2,1)}, u32[]{:S(2)}) copy-start(bf16[128,1024]{1,0:T(8,128)(2,1)} %refs_1_.1) | copy-start | bytes 786436
  0.7 21.0 %copy-start.1 = (bf16[128,1024]{1,0:T(8,128)(2,1)S(1)}, bf16[128,1024]{1,0:T(8,128)(2,1)}, u32[]{:S(2)}) copy-start(bf16[128,1024]{1,0:T(8,128)(2,1)} %refs_5_.1) | copy-start | bytes 786436
  4.1 34.3 %copy-start.3 = (f32[1024]{0:T(1024)S(1)}, f32[1024]{0:T(1024)}, u32[]{:S(2)}) copy-start(f32[1024]{0:T(1024)} %param.12) | copy-start | bytes 12292
  4.2 6.4 %collective-permute-start = (bf16[1024,256]{1,0:T(8,128)(2,1)S(1)}, bf16[1024,256]{1,0:T(8,128)(2,1)S(1)}, u32[]{:S(2)}, u32[]{:S(2)}) collective-permute-start(bf16[1024,256]{1,0:T(8,128)(2,1)S(1)} %bitcast.216), channel_id=1, source_target_pairs={{0,8},{8,0},{16,24},{24,16},{1,9},{9,1},{17,25},{25,17},{2,10},{10... | collective-permute-start | bytes 1572872 | tf_op jit(solution)/shard_map/ppermute | solution.py:240
  4.7 15.1 %collective-permute-start.1 = (bf16[1024,256]{1,0:T(8,128)(2,1)S(1)}, bf16[1024,256]{1,0:T(8,128)(2,1)S(1)}, u32[]{:S(2)}, u32[]{:S(2)}) collective-permute-start(bf16[1024,256]{1,0:T(8,128)(2,1)S(1)} %bitcast.217), channel_id=1, source_target_pairs={{0,16},{8,24},{16,0},{24,8},{1,17},{9,25},{17,1},{25,9},{2,18},{10... | collective-permute-start | bytes 1572872 | tf_op jit(solution)/shard_map/ppermute | solution.py:239
  19.8 1.9 %collective-permute-start.2 = (bf16[1024,256]{1,0:T(8,128)(2,1)S(1)}, bf16[1024,256]{1,0:T(8,128)(2,1)S(1)}, u32[]{:S(2)}, u32[]{:S(2)}) collective-permute-start(bf16[1024,256]{1,0:T(8,128)(2,1)S(1)} %collective-permute-done.1.refs_6_), channel_id=1, source_target_pairs={{0,8},{8,0},{16,24},{24,16},{1,9},{9,1},{17,25},{25,17},{2,10},{10... | collective-permute-start | bytes 1572872 | tf_op jit(solution)/shard_map/ppermute | solution.py:245
  28.5 8.4 %collective-permute-start.4 = (bf16[128,1024]{1,0:T(8,128)(2,1)S(1)}, bf16[128,1024]{1,0:T(8,128)(2,1)S(1)}, u32[]{:S(2)}, u32[]{:S(2)}) collective-permute-start(bf16[128,1024]{1,0:T(8,128)(2,1)S(1)} %shard_map.105.refs_2_), channel_id=1, source_target_pairs={{0,16},{8,24},{16,0},{24,8},{1,17},{9,25},{17,1},{25,9},{2,18},{10... | collective-permute-start | bytes 786440 | tf_op jit(solution)/shard_map/ppermute | solution.py:239
  30.3 6.7 %collective-permute-start.3 = (bf16[128,1024]{1,0:T(8,128)(2,1)S(1)}, bf16[128,1024]{1,0:T(8,128)(2,1)S(1)}, u32[]{:S(2)}, u32[]{:S(2)}) collective-permute-start(bf16[128,1024]{1,0:T(8,128)(2,1)S(1)} %shard_map.105.refs_2_), channel_id=1, source_target_pairs={{0,8},{8,0},{16,24},{24,16},{1,9},{9,1},{17,25},{25,17},{2,10},{10... | collective-permute-start | bytes 786440 | tf_op jit(solution)/shard_map/ppermute | solution.py:240
  36.9 1.5 %collective-permute-start.5 = (bf16[128,1024]{1,0:T(8,128)(2,1)S(1)}, bf16[128,1024]{1,0:T(8,128)(2,1)S(1)}, u32[]{:S(2)}, u32[]{:S(2)}) collective-permute-start(bf16[128,1024]{1,0:T(8,128)(2,1)S(1)} %collective-permute-done.4.refs_4_), channel_id=1, source_target_pairs={{0,8},{8,0},{16,24},{24,16},{1,9},{9,1},{17,25},{25,17},{2,10},{10... | collective-permute-start | bytes 786440 | tf_op jit(solution)/shard_map/ppermute | solution.py:245
  44.6 20.5 %collective-permute-start.6 = (bf16[2,4,64,768]{3,2,1,0:T(8,128)(2,1)S(1)}, bf16[2,4,64,768]{3,2,1,0:T(8,128)(2,1)S(1)}, u32[]{:S(2)}, u32[]{:S(2)}) collective-permute-start(bf16[2,4,64,768]{3,2,1,0:T(8,128)(2,1)S(1)} %shard_map.107), channel_id=1, source_target_pairs={{0,1},{1,0},{2,3},{3,2},{4,5},{5,4},{6,7},{7,6},{8,9},{9,8},{10,11... | collective-permute-start | bytes 2359304 | tf_op jit(solution)/shard_map/ppermute | solution.py:345
  50.4 21.6 %collective-permute-start.10 = (bf16[2,4,64,768]{3,2,1,0:T(8,128)(2,1)S(1)}, bf16[2,4,64,768]{3,2,1,0:T(8,128)(2,1)S(1)}, u32[]{:S(2)}, u32[]{:S(2)}) collective-permute-start(bf16[2,4,64,768]{3,2,1,0:T(8,128)(2,1)S(1)} %shard_map.108), channel_id=1, source_target_pairs={{0,2},{1,3},{2,0},{3,1},{4,6},{5,7},{6,4},{7,5},{8,10},{9,11},{10,... | collective-permute-start | bytes 2359304 | tf_op jit(solution)/shard_map/ppermute | solution.py:345
  56.1 25.8 %collective-permute-start.9 = (bf16[2,4,64,768]{3,2,1,0:T(8,128)(2,1)S(1)}, bf16[2,4,64,768]{3,2,1,0:T(8,128)(2,1)S(1)}, u32[]{:S(2)}, u32[]{:S(2)}) collective-permute-start(bf16[2,4,64,768]{3,2,1,0:T(8,128)(2,1)S(1)} %shard_map.109), channel_id=1, source_target_pairs={{0,1},{1,0},{2,3},{3,2},{4,5},{5,4},{6,7},{7,6},{8,9},{9,8},{10,11... | collective-permute-start | bytes 2359304 | tf_op jit(solution)/shard_map/ppermute | solution.py:345
  59.6 31.0 %collective-permute-start.8 = (bf16[2,4,64,512]{3,2,1,0:T(8,128)(2,1)S(1)}, bf16[2,4,64,512]{3,2,1,0:T(8,128)(2,1)S(1)}, u32[]{:S(2)}, u32[]{:S(2)}) collective-permute-start(bf16[2,4,64,512]{3,2,1,0:T(8,128)(2,1)S(1)} %shard_map.110), channel_id=1, source_target_pairs={{0,2},{1,3},{2,0},{3,1},{4,6},{5,7},{6,4},{7,5},{8,10},{9,11},{10,... | collective-permute-start | bytes 1572872 | tf_op jit(solution)/shard_map/ppermute | solution.py:345
  62.7 32.5 %collective-permute-start.7 = (bf16[2,4,64,512]{3,2,1,0:T(8,128)(2,1)S(1)}, bf16[2,4,64,512]{3,2,1,0:T(8,128)(2,1)S(1)}, u32[]{:S(2)}, u32[]{:S(2)}) collective-permute-start(bf16[2,4,64,512]{3,2,1,0:T(8,128)(2,1)S(1)} %shard_map.111), channel_id=1, source_target_pairs={{0,1},{1,0},{2,3},{3,2},{4,5},{5,4},{6,7},{7,6},{8,9},{9,8},{10,11... | collective-permute-start | bytes 1572872 | tf_op jit(solution)/shard_map/ppermute | solution.py:345
  69.2 29.8 %collective-permute-start.11 = (bf16[2,2,64,768]{3,2,0,1:T(8,128)(2,1)S(1)}, bf16[2,2,64,768]{3,2,0,1:T(8,128)(2,1)S(1)}, u32[]{:S(2)}, u32[]{:S(2)}) collective-permute-start(bf16[2,2,64,768]{3,2,0,1:T(8,128)(2,1)S(1)} %bitcast.232), channel_id=1, source_target_pairs={{0,4},{1,5},{2,6},{3,7},{4,0},{5,1},{6,2},{7,3},{8,12},{9,13},{10,... | collective-permute-start | bytes 1179656 | tf_op jit(solution)/shard_map/ppermute | solution.py:345
  76.2 25.5 %collective-permute-start.13 = (bf16[2,2,64,768]{3,2,0,1:T(8,128)(2,1)S(1)}, bf16[2,2,64,768]{3,2,0,1:T(8,128)(2,1)S(1)}, u32[]{:S(2)}, u32[]{:S(2)}) collective-permute-start(bf16[2,2,64,768]{3,2,0,1:T(8,128)(2,1)S(1)} %bitcast.231), channel_id=1, source_target_pairs={{0,1},{1,0},{2,3},{3,2},{4,5},{5,4},{6,7},{7,6},{8,9},{9,8},{10,11... | collective-permute-start | bytes 1179656 | tf_op jit(solution)/shard_map/ppermute | solution.py:345
  81.9 21.6 %collective-permute-start.12 = (bf16[2,4,64,256]{3,2,1,0:T(8,128)(2,1)S(1)}, bf16[2,4,64,256]{3,2,1,0:T(8,128)(2,1)S(1)}, u32[]{:S(2)}, u32[]{:S(2)}) collective-permute-start(bf16[2,4,64,256]{3,2,1,0:T(8,128)(2,1)S(1)} %shard_map.114), channel_id=1, source_target_pairs={{0,2},{1,3},{2,0},{3,1},{4,6},{5,7},{6,4},{7,5},{8,10},{9,11},{10,... | collective-permute-start | bytes 786440 | tf_op jit(solution)/shard_map/ppermute | solution.py:345
  90.6 18.7 %collective-permute-start.14 = (bf16[2,2,64,768]{3,2,1,0:T(8,128)(2,1)S(1)}, bf16[2,2,64,768]{3,2,1,0:T(8,128)(2,1)S(1)}, u32[]{:S(2)}, u32[]{:S(2)}) collective-permute-start(bf16[2,2,64,768]{3,2,1,0:T(8,128)(2,1)S(1)} %bitcast.225), channel_id=1, source_target_pairs={{0,4},{1,5},{2,6},{3,7},{4,0},{5,1},{6,2},{7,3},{8,12},{9,13},{10,... | collective-permute-start | bytes 1179656 | tf_op jit(solution)/shard_map/ppermute | solution.py:345
  95.2 14.8 %collective-permute-start.15 = (bf16[2,2,64,512]{3,2,0,1:T(8,128)(2,1)S(1)}, bf16[2,2,64,512]{3,2,0,1:T(8,128)(2,1)S(1)}, u32[]{:S(2)}, u32[]{:S(2)}) collective-permute-start(bf16[2,2,64,512]{3,2,0,1:T(8,128)(2,1)S(1)} %bitcast.233), channel_id=1, source_target_pairs={{0,1},{1,0},{2,3},{3,2},{4,5},{5,4},{6,7},{7,6},{8,9},{9,8},{10,11... | collective-permute-start | bytes 786440 | tf_op jit(solution)/shard_map/ppermute | solution.py:345
  99.0 14.6 %collective-permute-start.17 = (bf16[2,2,64,512]{3,2,1,0:T(8,128)(2,1)S(1)}, bf16[2,2,64,512]{3,2,1,0:T(8,128)(2,1)S(1)}, u32[]{:S(2)}, u32[]{:S(2)}) collective-permute-start(bf16[2,2,64,512]{3,2,1,0:T(8,128)(2,1)S(1)} %bitcast.226), channel_id=1, source_target_pairs={{0,2},{1,3},{2,0},{3,1},{4,6},{5,7},{6,4},{7,5},{8,10},{9,11},{10,... | collective-permute-start | bytes 786440 | tf_op jit(solution)/shard_map/ppermute | solution.py:345
  101.7 23.9 %collective-permute-start.20 = (bf16[2,1,64,768]{3,2,0,1:T(8,128)(2,1)S(1)}, bf16[2,1,64,768]{3,2,0,1:T(8,128)(2,1)S(1)}, u32[]{:S(2)}, u32[]{:S(2)}) collective-permute-start(bf16[2,1,64,768]{3,2,0,1:T(8,128)(2,1)S(1)} %get-tuple-element.110), channel_id=1, source_target_pairs={{0,2},{1,3},{2,0},{3,1},{4,6},{5,7},{6,4},{7,5},{8,10},{9,11},{10,... | collective-permute-start | bytes 589832 | tf_op jit(solution)/shard_map/ppermute | solution.py:345
  105.7 11.5 %collective-permute-start.18 = (bf16[2,2,64,256]{3,2,1,0:T(8,128)(2,1)S(1)}, bf16[2,2,64,256]{3,2,1,0:T(8,128)(2,1)S(1)}, u32[]{:S(2)}, u32[]{:S(2)}) collective-permute-start(bf16[2,2,64,256]{3,2,1,0:T(8,128)(2,1)S(1)} %bitcast.227), channel_id=1, source_target_pairs={{0,1},{1,0},{2,3},{3,2},{4,5},{5,4},{6,7},{7,6},{8,9},{9,8},{10,11... | collective-permute-start | bytes 393224 | tf_op jit(solution)/shard_map/ppermute | solution.py:345
  109.3 17.5 %collective-permute-start.22 = (bf16[2,1,64,768]{3,2,0,1:T(8,128)(2,1)S(1)}, bf16[2,1,64,768]{3,2,0,1:T(8,128)(2,1)S(1)}, u32[]{:S(2)}, u32[]{:S(2)}) collective-permute-start(bf16[2,1,64,768]{3,2,0,1:T(8,128)(2,1)S(1)} %get-tuple-element.108), channel_id=1, source_target_pairs={{0,4},{1,5},{2,6},{3,7},{4,0},{5,1},{6,2},{7,3},{8,12},{9,13},{10,... | collective-permute-start | bytes 589832 | tf_op jit(solution)/shard_map/ppermute | solution.py:345
  110.0 3.7 %collective-permute-start.16 = (f32[4,64]{1,0:T(4,128)S(1)}, f32[4,64]{1,0:T(4,128)S(1)}, u32[]{:S(2)}, u32[]{:S(2)}) collective-permute-start(f32[4,64]{1,0:T(4,128)S(1)} %bitcast.237), channel_id=1, source_target_pairs={{0,1},{1,0},{2,3},{3,2},{4,5},{5,4},{6,7},{7,6},{8,9},{9,8},{10,11... | collective-permute-start | bytes 3080 | tf_op jit(solution)/shard_map/ppermute | solution.py:345
  113.8 4.9 %collective-permute-start.19 = (f32[2,64]{1,0:T(2,128)S(1)}, f32[2,64]{1,0:T(2,128)S(1)}, u32[]{:S(2)}, u32[]{:S(2)}) collective-permute-start(f32[2,64]{1,0:T(2,128)S(1)} %bitcast.240), channel_id=1, source_target_pairs={{0,2},{1,3},{2,0},{3,1},{4,6},{5,7},{6,4},{7,5},{8,10},{9,11},{10,... | collective-permute-start | bytes 1544 | tf_op jit(solution)/shard_map/ppermute | solution.py:345
  118.7 4.9 %collective-permute-start.21 = (f32[1,64]{1,0:T(1,128)S(1)}, f32[1,64]{1,0:T(1,128)S(1)}, u32[]{:S(2)}, u32[]{:S(2)}) collective-permute-start(f32[1,64]{1,0:T(1,128)S(1)} %slice_bitcast_fusion.24), channel_id=1, source_target_pairs={{0,4},{1,5},{2,6},{3,7},{4,0},{5,1},{6,2},{7,3},{8,12},{9,13},{10,... | collective-permute-start | bytes 776 | tf_op jit(solution)/shard_map/ppermute | solution.py:345
  120.6 8.5 %collective-permute-start.23 = (bf16[2,1,64,768]{3,2,0,1:T(8,128)(2,1)S(1)}, bf16[2,1,64,768]{3,2,0,1:T(8,128)(2,1)S(1)}, u32[]{:S(2)}, u32[]{:S(2)}) collective-permute-start(bf16[2,1,64,768]{3,2,0,1:T(8,128)(2,1)S(1)} %get-tuple-element.106), channel_id=1, source_target_pairs={{0,2},{1,3},{2,0},{3,1},{4,6},{5,7},{6,4},{7,5},{8,10},{9,11},{10,... | collective-permute-start | bytes 589832 | tf_op jit(solution)/shard_map/ppermute | solution.py:345
  122.7 11.8 %collective-permute-start.24 = (bf16[2,1,64,512]{3,2,0,1:T(8,128)(2,1)S(1)}, bf16[2,1,64,512]{3,2,0,1:T(8,128)(2,1)S(1)}, u32[]{:S(2)}, u32[]{:S(2)}) collective-permute-start(bf16[2,1,64,512]{3,2,0,1:T(8,128)(2,1)S(1)} %get-tuple-element.114), channel_id=1, source_target_pairs={{0,4},{1,5},{2,6},{3,7},{4,0},{5,1},{6,2},{7,3},{8,12},{9,13},{10,... | collective-permute-start | bytes 393224 | tf_op jit(solution)/shard_map/ppermute | solution.py:345
  123.6 12.2 %collective-permute-start.25 = (bf16[2,1,64,512]{3,2,0,1:T(8,128)(2,1)S(1)}, bf16[2,1,64,512]{3,2,0,1:T(8,128)(2,1)S(1)}, u32[]{:S(2)}, u32[]{:S(2)}) collective-permute-start(bf16[2,1,64,512]{3,2,0,1:T(8,128)(2,1)S(1)} %get-tuple-element.112), channel_id=1, source_target_pairs={{0,4},{1,5},{2,6},{3,7},{4,0},{5,1},{6,2},{7,3},{8,12},{9,13},{10,... | collective-permute-start | bytes 393224 | tf_op jit(solution)/shard_map/ppermute | solution.py:345
  125.6 11.0 %collective-permute-start.26 = (bf16[2,1,64,256]{3,2,0,1:T(8,128)(2,1)S(1)}, bf16[2,1,64,256]{3,2,0,1:T(8,128)(2,1)S(1)}, u32[]{:S(2)}, u32[]{:S(2)}) collective-permute-start(bf16[2,1,64,256]{3,2,0,1:T(8,128)(2,1)S(1)} %get-tuple-element.116), channel_id=1, source_target_pairs={{0,4},{1,5},{2,6},{3,7},{4,0},{5,1},{6,2},{7,3},{8,12},{9,13},{10,... | collective-permute-start | bytes 196616 | tf_op jit(solution)/shard_map/ppermute | solution.py:345
  136.7 0.8 copy-start.4
